TPU v7x, 32 devices: a whole 2x2x4 slice. The times are simulated.
32 devices in a mesh: groups: 2 (over x), slab: 16 (over z, y, core).
Axes of the slice: x: 2, y: 2, z: 4, core: 2. Of those that a mesh axis runs over, the one named last changes fastest.
Arguments:
- point_pos: float32 [3, 131072], P(None, ('groups', 'slab')), parts along dimension 1, may hold values from 0 to 1
- point_input: float32 [8, 131072], P(None, ('groups', 'slab')), parts along dimension 1, may hold values from -6 to 6
- req_owner: int32 [16384, 1], P(('groups', 'slab')), parts along dimension 0, may hold values from 0 to 15; in each aligned block of 512 rows (0 to 511, 512 to 1023, ...) at most 128 rows name the same one
- req_local: int32 [16384], P(('groups', 'slab')), parts along dimension 0, may hold values from 0 to 4095
- pair_cell: int32 [128], P(('groups', 'slab')), parts along dimension 0, may hold values from 0 to 1
- pair_mask: int32 [128, 64, 128], P(('groups', 'slab')), parts along dimension 0, may hold values 0 or 1
- w_first: float32 [7, 256], replicated, may hold values from -2.5 to 2.5
- w_second: bfloat16 [256, 64], replicated, may hold values from -1.5 to 1.5
- w_lift: float32 [8, 64], replicated, may hold values from -2 to 2
- cotangent: float32 [64, 4096], P(None, ('groups', 'slab')), parts along dimension 1, may hold values from -6 to 6
Outputs:
- latent: bfloat16 [64, 4096], P(None, ('groups', 'slab')), parts along dimension 1
- grad_first: float32 [14, 256], P('groups'), parts along dimension 0
- grad_second: float32 [512, 64], P('groups'), parts along dimension 0
- grad_lift: float32 [16, 64], P('groups'), parts along dimension 0
There are 2 independent parts, one for each index of `groups`. A program takes and returns all parts, laid end to end along the dimension named above; an argument that names none is the same for every part. Nothing has to cross between parts.
Inputs may be any that keep to these rules, and one draw needn't show every extreme that they name: `req_owner`: within the 512 rows of one slab (aligned blocks), no partition is named more than 128 times.
All inputs are finite; a program needn't handle non-finite values. No bound on the sum of `pair_mask` on one device may be relied on, other than what follows from the above.
Results may differ from a plain program's by a relative error of at most 0.0034.
Values sent between devices are 32-bit elements; how exact they have to be, the bound alone decides.
A program may use at most 64 MiB of HBM per device.

v0:
```python
import jax
import jax.numpy as jnp
from jax import lax
from jax.sharding import PartitionSpec as P

BLOCK_PTS = 128
BLOCK_CELLS = 64
GRID_ROW = 16


PREC = lax.Precision.HIGHEST


def silu_slope(values):
    sig = jax.nn.sigmoid(values)
    return sig * (1.0 + values * (1.0 - sig))


def cell_coords(local, slab_id, cells_dev, slab_count, grid_row):
    column = (local % grid_row).astype(jnp.float32)
    row_idx = (local // grid_row).astype(jnp.float32)
    first = (column + 0.5) / grid_row
    second = (row_idx + 0.5) * grid_row / cells_dev
    third = (slab_id.astype(jnp.float32) + 0.5) / slab_count + 0.0 * first
    return jnp.stack([first, second, third])


def pair_terms(points_y, feats, cells_x, mask, gcell, w_first, w_second):
    point_part = jnp.dot(
        points_y.T, w_first[0:3], precision=PREC, preferred_element_type=jnp.float32
    )
    cell_part = (
        jnp.dot(cells_x.T, w_first[3:6], precision=PREC, preferred_element_type=jnp.float32)
        + w_first[6]
    )
    n_cells = cell_part.shape[0]
    n_points = point_part.shape[0]
    width = point_part.shape[1]
    preact = (cell_part[:, None, :] + point_part[None, :, :]).reshape(n_cells * n_points, width)
    activ, slope_fn = jax.vjp(jax.nn.gelu, preact)
    hidden = activ.astype(jnp.bfloat16)
    kernel = lax.dot_general(
        w_second, hidden, (((0,), (1,)), ((), ())), preferred_element_type=jnp.float32
    )
    kernel = kernel.reshape(-1, n_cells, n_points)
    weighted = mask[None, :, :] * feats[:, None, :]
    contrib = jnp.sum(kernel * weighted, axis=2)
    dkernel = (weighted * gcell[:, :, None]).astype(jnp.bfloat16).reshape(-1, n_cells * n_points)
    dfeat = jnp.sum(kernel * mask[None, :, :] * gcell[:, :, None], axis=1)
    dsecond = lax.dot_general(
        hidden, dkernel, (((0,), (1,)), ((), ())), preferred_element_type=jnp.float32
    )
    dhidden = lax.dot_general(
        dkernel, w_second, (((0,), (1,)), ((), ())), preferred_element_type=jnp.float32
    )
    dpre = slope_fn(dhidden)[0].reshape(n_cells, n_points, width)
    per_point = jnp.sum(dpre, axis=0)
    per_cell = jnp.sum(dpre, axis=1)
    dfirst = jnp.concatenate(
        [
            jnp.dot(points_y, per_point, precision=PREC, preferred_element_type=jnp.float32),
            jnp.dot(cells_x, per_cell, precision=PREC, preferred_element_type=jnp.float32),
            jnp.sum(per_cell, axis=0, keepdims=True),
        ],
        axis=0,
    )
    return (contrib, dfeat, dfirst, dsecond)


def per_device(
    point_pos,
    point_input,
    req_owner,
    req_local,
    pair_cell,
    pair_mask,
    w_first,
    w_second,
    w_lift,
    cotangent,
):
    peers = lax.axis_size("slab")
    slab_index = lax.axis_index("slab")
    req_count = req_local.shape[0]
    capacity = 4 * req_count // peers
    owners = req_owner[:, 0]
    onehot = (owners[:, None] == jnp.arange(peers, dtype=jnp.int32)[None, :]).astype(jnp.int32)
    ranks = jnp.sum(jnp.cumsum(onehot, axis=0) * onehot, axis=1) - 1
    slots = owners * capacity + ranks
    wanted = jnp.zeros((peers * capacity,), jnp.int32).at[slots].set(req_local)
    asked = lax.all_to_all(wanted, "slab", split_axis=0, concat_axis=0, tiled=True)
    sent_pos = point_pos[:, asked]
    sent_input = point_input[:, asked]
    sent_z = jnp.dot(w_lift.T, sent_input, precision=PREC, preferred_element_type=jnp.float32)
    sent_feat = jax.nn.silu(sent_z)
    got_pos, got_feat = (
        lax.all_to_all(sent_pos, "slab", split_axis=1, concat_axis=1, tiled=True),
        lax.all_to_all(sent_feat, "slab", split_axis=1, concat_axis=1, tiled=True),
    )
    req_pos = got_pos[:, slots]
    req_feat = got_feat[:, slots]
    mask_float = pair_mask.astype(jnp.float32)
    pair_count = pair_mask.shape[0]
    block_count = cotangent.shape[1] // BLOCK_CELLS
    select = (pair_cell[:, None] == jnp.arange(block_count, dtype=jnp.int32)[None, :]).astype(
        jnp.float32
    )
    counts = jnp.einsum("pb,pc->bc", select, jnp.sum(mask_float, axis=2), precision=PREC)
    divisor = jnp.maximum(counts, 1.0)
    channel_count = cotangent.shape[0]
    gcells = cotangent.reshape(channel_count, block_count, BLOCK_CELLS) / divisor[None, :, :]
    local_cells = jnp.arange(block_count * BLOCK_CELLS, dtype=jnp.int32)
    cells_here = cell_coords(local_cells, slab_index, block_count * BLOCK_CELLS, peers, GRID_ROW)
    cells_here = cells_here.reshape(3, block_count, BLOCK_CELLS)
    pair_pos = req_pos.reshape(3, pair_count, BLOCK_PTS).transpose(1, 0, 2)
    pair_feat = req_feat.reshape(channel_count, pair_count, BLOCK_PTS).transpose(1, 0, 2)
    pair_cells = cells_here[:, pair_cell].transpose(1, 0, 2)
    pair_grads = gcells[:, pair_cell].transpose(1, 0, 2)

    def per_pair(pieces):
        return pair_terms(pieces[0], pieces[1], pieces[2], pieces[3], pieces[4], w_first, w_second)

    contrib, dfeat, dfirst, dsecond = lax.map(
        per_pair, (pair_pos, pair_feat, pair_cells, mask_float, pair_grads)
    )
    summed = jnp.einsum("pb,pkc->kbc", select, contrib, precision=PREC)
    latent = (
        (summed / divisor[None, :, :])
        .reshape(channel_count, block_count * BLOCK_CELLS)
        .astype(jnp.bfloat16)
    )
    req_grad = dfeat.transpose(1, 0, 2).reshape(channel_count, pair_count * BLOCK_PTS)
    outbound = jnp.zeros((channel_count, peers * capacity), jnp.float32).at[:, slots].set(req_grad)
    returned = lax.all_to_all(outbound, "slab", split_axis=1, concat_axis=1, tiled=True)
    lift_part = jnp.dot(
        sent_input,
        (returned * silu_slope(sent_z)).T,
        precision=PREC,
        preferred_element_type=jnp.float32,
    )
    grad_first, grad_second, grad_lift = lax.psum(
        (jnp.sum(dfirst, axis=0), jnp.sum(dsecond, axis=0), lift_part), "slab"
    )
    return (latent, grad_first, grad_second, grad_lift)


def solution(mesh):
    in_specs = (
        P(None, ("groups", "slab")),
        P(None, ("groups", "slab")),
        P(("groups", "slab"), None),
        P(("groups", "slab")),
        P(("groups", "slab")),
        P(("groups", "slab"), None, None),
        P(),
        P(),
        P(),
        P(None, ("groups", "slab")),
    )
    out_specs = (
        P(None, ("groups", "slab")),
        P("groups", None),
        P("groups", None),
        P("groups", None),
    )
    return jax.shard_map(
        per_device, mesh=mesh, in_specs=in_specs, out_specs=out_specs, check_vma=False
    )
```

profile of v0, /device:TPU:0, one launch (start us, length us, event | category | flops | bytes accessed | tf_op | source)
XLA Modules:
  0.0 331.7 jit_solution(16420068045337851878)
XLA Ops:
  10.8 3.2 scatter_custom_fusion
  14.0 7.4 %all-to-all-start = ((s32[16,128,1]{1,2,0:T(1,128)}), s32[16,128,1]{1,2,0:T(1,128)S(1)}, u32[]{:S(2)}, u32[]{:S(2)}) async-start(s32[16,128,1]{1,2,0:T(1,128)} %bitcast.22), calls=%async_computation | async-start | bytes 16384 | tf_op jit(solution)/shard_map/all_to_all | solution.py:91
  24.1 2.8 copy.39
  26.9 1.5 copy.43
  29.4 7.1 %gather_fusion.1 = f32[2048,3]{1,0:T(8,128)S(1)} fusion(f32[3,4096]{0,1:T(8,128)} %copy.39, s32[2048]{0:T(1024)S(1)} %broadcast_clamp_fusion), kind=kCustom, calls=%fused_computation.1 | custom fusion | bytes 57344 | tf_op jit(solution)/shard_map/gather | solution.py:92
  37.4 6.0 %all-to-all-start.1 = ((f32[3,16,128]{2,0,1:T(4,128)}), f32[3,16,128]{2,0,1:T(4,128)S(1)}, u32[]{:S(2)}, u32[]{:S(2)}) async-start(f32[3,16,128]{2,0,1:T(4,128)} %copy.40), calls=%async_computation.1 | async-start | bytes 65536 | tf_op jit(solution)/shard_map/all_to_all | solution.py:97
  43.4 5.5 %gather_fusion.3 = f32[2048,8]{1,0:T(8,128)S(1)} fusion(f32[8,4096]{0,1:T(8,128)S(1)} %copy.43, s32[2048]{0:T(1024)S(1)} %broadcast_clamp_fusion), kind=kCustom, calls=%fused_computation.3 | custom fusion | bytes 139264 | tf_op jit(solution)/shard_map/gather | solution.py:93
  51.9 6.0 %all-to-all-start.2 = ((f32[64,16,128]{2,0,1:T(8,128)}), f32[64,16,128]{2,0,1:T(8,128)S(1)}, u32[]{:S(2)}, u32[]{:S(2)}) async-start(f32[64,16,128]{2,0,1:T(8,128)} %copy_bitcast_fusion), calls=%async_computation.2 | async-start | bytes 1048576 | tf_op jit(solution)/shard_map/all_to_all | solution.py:98
  60.8 11.7 %all-to-all-done.2 = f32[64,16,128]{2,0,1:T(8,128)S(1)} async-done(((f32[64,16,128]{2,0,1:T(8,128)}), f32[64,16,128]{2,0,1:T(8,128)S(1)}, u32[]{:S(2)}, u32[]{:S(2)}) %all-to-all-start.2) | async-done | bytes 524320 | tf_op jit(solution)/shard_map/all_to_all | solution.py:98
  74.0 150.2 %while.18 = (s32[]{:T(128)}, f32[4,64,64]{2,0,1:T(4,128)}, f32[4,64,128]{2,1,0:T(8,128)}, f32[4,7,256]{2,1,0:T(8,128)S(1)}, f32[4,256,64]{1,2,0:T(8,128)}, /*ind...) while((s32[]{:T(128)}, f32[4,64,64]{2,0,1:T(4,128)}, ...), condition=%wide.region_11.12_spmd, body=%wide.region_5.11_spmd.sunk | while | flops 894262528 | bytes 165244144 | solution.py:123
  75.9 5.7 %fusion.112 = (f32[8192,256]{1,0:T(8,128)}, bf16[8192,256]{1,0:T(8,128)(2,1)S(1)}) fusion(f32[64,128,256]{2,1,0:T(8,128)S(1)} %broadcast_add_fusion.3), kind=kLoop, calls=%fused_computation.17.clone.2 | loop fusion | flops 18874368 | bytes 20971520 | tf_op jit(solution)/shard_map/while/body/eval_jaxpr/jvp()/tanh | solution.py:40
  81.6 1.4 convolution_bitcast_fusion.4
  83.4 1.5 multiply_reduce_fusion.2
  85.0 1.7 dynamic_update_slice.38
  88.0 11.3 %fusion.113 = (f32[256]{0:T(256)S(1)}, f32[8192,256]{1,0:T(8,128)S(1)}) fusion(f32[8192,256]{1,0:T(8,128)} %get-tuple-element.295, f32[64,128,256]{2,1,0:T(8,128)} %copy-done.1, bf16[256,64]{0,1:T(8,128)(2,1)S(1)} %get-tuple-element.338, f32[8,8,64,128]{3,2,1,0:T(8,128)S(1)} %bitcast.213, f32[8,8,64,128]{3,2,1,0:T(8,128)S(1)} %bitcast.214, ...), kind=kOutput, calls=%fused_computation.125.clone.1 | convolution fusion | flops 303562496 | bytes 29426688 | tf_op jit(solution)/shard_map/while/body/eval_jaxpr/dot_general | solution.py:53
  99.3 3.2 copy-done.2
  103.7 3.9 %reduce_sum.113 = f32[128,256]{1,0:T(8,128)S(1)} reduce(f32[64,128,256]{2,1,0:T(8,128)} %bitcast.211, f32[]{:T(128)} %constant.129.clone.1..sunk), dimensions={0}, to_apply=%region_8.8 | reduce | flops 2064384 | bytes 8519684 | tf_op jit(solution)/shard_map/while/body/eval_jaxpr/reduce_sum | solution.py:57
  107.8 3.9 %fusion.117 = f32[4,256,64]{1,2,0:T(8,128)} fusion(f32[4,256,64]{1,2,0:T(8,128)} %get-tuple-element.319, s32[]{:T(128)S(6)} %copy.99, f32[128,256]{1,0:T(8,128)S(1)} %fusion.111, f32[64,256]{1,0:T(8,128)S(1)} %convolution_add_fusion.2, bf16[64,64,128]{2,1,0:T(8,128)(2,1)S(1)} %get-tuple-element.299), kind=kOutput, calls=%fused_computation.44.clone.1 | convolution fusion | flops 289406976 | bytes 1310724 | tf_op jit(solution)/shard_map/while/body/eval_jaxpr/dot_general | solution.py:50
  113.4 5.7 %fusion.112 = (f32[8192,256]{1,0:T(8,128)}, bf16[8192,256]{1,0:T(8,128)(2,1)S(1)}) fusion(f32[64,128,256]{2,1,0:T(8,128)S(1)} %broadcast_add_fusion.3), kind=kLoop, calls=%fused_computation.17.clone.2 | loop fusion | flops 18874368 | bytes 20971520 | tf_op jit(solution)/shard_map/while/body/eval_jaxpr/jvp()/tanh | solution.py:40
  120.9 1.5 multiply_reduce_fusion.2
  122.5 1.7 dynamic_update_slice.38
  125.5 11.3 %fusion.113 = (f32[256]{0:T(256)S(1)}, f32[8192,256]{1,0:T(8,128)S(1)}) fusion(f32[8192,256]{1,0:T(8,128)} %get-tuple-element.295, f32[64,128,256]{2,1,0:T(8,128)} %copy-done.1, bf16[256,64]{0,1:T(8,128)(2,1)S(1)} %get-tuple-element.338, f32[8,8,64,128]{3,2,1,0:T(8,128)S(1)} %bitcast.213, f32[8,8,64,128]{3,2,1,0:T(8,128)S(1)} %bitcast.214, ...), kind=kOutput, calls=%fused_computation.125.clone.1 | convolution fusion | flops 303562496 | bytes 29426688 | tf_op jit(solution)/shard_map/while/body/eval_jaxpr/dot_general | solution.py:53
  136.8 3.2 copy-done.2
  141.2 3.9 %reduce_sum.113 = f32[128,256]{1,0:T(8,128)S(1)} reduce(f32[64,128,256]{2,1,0:T(8,128)} %bitcast.211, f32[]{:T(128)} %constant.129.clone.1..sunk), dimensions={0}, to_apply=%region_8.8 | reduce | flops 2064384 | bytes 8519684 | tf_op jit(solution)/shard_map/while/body/eval_jaxpr/reduce_sum | solution.py:57
  145.3 3.9 %fusion.117 = f32[4,256,64]{1,2,0:T(8,128)} fusion(f32[4,256,64]{1,2,0:T(8,128)} %get-tuple-element.319, s32[]{:T(128)S(6)} %copy.99, f32[128,256]{1,0:T(8,128)S(1)} %fusion.111, f32[64,256]{1,0:T(8,128)S(1)} %convolution_add_fusion.2, bf16[64,64,128]{2,1,0:T(8,128)(2,1)S(1)} %get-tuple-element.299), kind=kOutput, calls=%fused_computation.44.clone.1 | convolution fusion | flops 289406976 | bytes 1310724 | tf_op jit(solution)/shard_map/while/body/eval_jaxpr/dot_general | solution.py:50
  150.9 5.7 %fusion.112 = (f32[8192,256]{1,0:T(8,128)}, bf16[8192,256]{1,0:T(8,128)(2,1)S(1)}) fusion(f32[64,128,256]{2,1,0:T(8,128)S(1)} %broadcast_add_fusion.3), kind=kLoop, calls=%fused_computation.17.clone.2 | loop fusion | flops 18874368 | bytes 20971520 | tf_op jit(solution)/shard_map/while/body/eval_jaxpr/jvp()/tanh | solution.py:40
  156.6 1.4 convolution_bitcast_fusion.4
  158.4 1.5 multiply_reduce_fusion.2
  160.0 1.7 dynamic_update_slice.38
  163.0 11.3 %fusion.113 = (f32[256]{0:T(256)S(1)}, f32[8192,256]{1,0:T(8,128)S(1)}) fusion(f32[8192,256]{1,0:T(8,128)} %get-tuple-element.295, f32[64,128,256]{2,1,0:T(8,128)} %copy-done.1, bf16[256,64]{0,1:T(8,128)(2,1)S(1)} %get-tuple-element.338, f32[8,8,64,128]{3,2,1,0:T(8,128)S(1)} %bitcast.213, f32[8,8,64,128]{3,2,1,0:T(8,128)S(1)} %bitcast.214, ...), kind=kOutput, calls=%fused_computation.125.clone.1 | convolution fusion | flops 303562496 | bytes 29426688 | tf_op jit(solution)/shard_map/while/body/eval_jaxpr/dot_general | solution.py:53
  174.3 3.2 copy-done.2
  178.7 3.9 %reduce_sum.113 = f32[128,256]{1,0:T(8,128)S(1)} reduce(f32[64,128,256]{2,1,0:T(8,128)} %bitcast.211, f32[]{:T(128)} %constant.129.clone.1..sunk), dimensions={0}, to_apply=%region_8.8 | reduce | flops 2064384 | bytes 8519684 | tf_op jit(solution)/shard_map/while/body/eval_jaxpr/reduce_sum | solution.py:57
  182.8 3.9 %fusion.117 = f32[4,256,64]{1,2,0:T(8,128)} fusion(f32[4,256,64]{1,2,0:T(8,128)} %get-tuple-element.319, s32[]{:T(128)S(6)} %copy.99, f32[128,256]{1,0:T(8,128)S(1)} %fusion.111, f32[64,256]{1,0:T(8,128)S(1)} %convolution_add_fusion.2, bf16[64,64,128]{2,1,0:T(8,128)(2,1)S(1)} %get-tuple-element.299), kind=kOutput, calls=%fused_computation.44.clone.1 | convolution fusion | flops 289406976 | bytes 1310724 | tf_op jit(solution)/shard_map/while/body/eval_jaxpr/dot_general | solution.py:50
  188.4 5.7 %fusion.112 = (f32[8192,256]{1,0:T(8,128)}, bf16[8192,256]{1,0:T(8,128)(2,1)S(1)}) fusion(f32[64,128,256]{2,1,0:T(8,128)S(1)} %broadcast_add_fusion.3), kind=kLoop, calls=%fused_computation.17.clone.2 | loop fusion | flops 18874368 | bytes 20971520 | tf_op jit(solution)/shard_map/while/body/eval_jaxpr/jvp()/tanh | solution.py:40
  195.9 1.5 multiply_reduce_fusion.2
  197.5 1.7 dynamic_update_slice.38
  200.5 11.3 %fusion.113 = (f32[256]{0:T(256)S(1)}, f32[8192,256]{1,0:T(8,128)S(1)}) fusion(f32[8192,256]{1,0:T(8,128)} %get-tuple-element.295, f32[64,128,256]{2,1,0:T(8,128)} %copy-done.1, bf16[256,64]{0,1:T(8,128)(2,1)S(1)} %get-tuple-element.338, f32[8,8,64,128]{3,2,1,0:T(8,128)S(1)} %bitcast.213, f32[8,8,64,128]{3,2,1,0:T(8,128)S(1)} %bitcast.214, ...), kind=kOutput, calls=%fused_computation.125.clone.1 | convolution fusion | flops 303562496 | bytes 29426688 | tf_op jit(solution)/shard_map/while/body/eval_jaxpr/dot_general | solution.py:53
  211.8 3.2 copy-done.2
  216.2 3.9 %reduce_sum.113 = f32[128,256]{1,0:T(8,128)S(1)} reduce(f32[64,128,256]{2,1,0:T(8,128)} %bitcast.211, f32[]{:T(128)} %constant.129.clone.1..sunk), dimensions={0}, to_apply=%region_8.8 | reduce | flops 2064384 | bytes 8519684 | tf_op jit(solution)/shard_map/while/body/eval_jaxpr/reduce_sum | solution.py:57
  220.3 3.9 %fusion.117 = f32[4,256,64]{1,2,0:T(8,128)} fusion(f32[4,256,64]{1,2,0:T(8,128)} %get-tuple-element.319, s32[]{:T(128)S(6)} %copy.99, f32[128,256]{1,0:T(8,128)S(1)} %fusion.111, f32[64,256]{1,0:T(8,128)S(1)} %convolution_add_fusion.2, bf16[64,64,128]{2,1,0:T(8,128)(2,1)S(1)} %get-tuple-element.299), kind=kOutput, calls=%fused_computation.44.clone.1 | convolution fusion | flops 289406976 | bytes 1310724 | tf_op jit(solution)/shard_map/while/body/eval_jaxpr/dot_general | solution.py:50
  225.3 2.1 scatter_custom_fusion.1
  228.5 4.1 %all-to-all-start.3 = ((f32[64,16,128]{2,0,1:T(8,128)}), f32[64,16,128]{2,0,1:T(8,128)S(1)}, u32[]{:S(2)}, u32[]{:S(2)}) async-start(f32[64,16,128]{2,0,1:T(8,128)} %copy.51), calls=%async_computation.3 | async-start | bytes 1048576 | tf_op jit(solution)/shard_map/all_to_all | solution.py:134
  234.5 1.6 reduce_sum.99
  236.1 10.9 %all-to-all-done.3 = f32[64,16,128]{2,0,1:T(8,128)S(1)} async-done(((f32[64,16,128]{2,0,1:T(8,128)}), f32[64,16,128]{2,0,1:T(8,128)S(1)}, u32[]{:S(2)}, u32[]{:S(2)}) %all-to-all-start.3) | async-done | bytes 524320 | tf_op jit(solution)/shard_map/all_to_all | solution.py:134
  247.0 3.0 fusion.45
  250.0 60.2 %all-reduce = (f32[7,256]{1,0:T(8,128)}, f32[8,64]{1,0:T(8,128)}) all-reduce(f32[7,256]{1,0:T(8,128)S(1)} %reduce_sum.98, f32[8,64]{1,0:T(8,128)S(1)} %fusion.45), channel_id=1, replica_groups=mesh['groups'=2,'slab'=16] {'slab'}, use_global_device_ids=true, to_apply=%region_13.14 | all-reduce | flops 2304 | bytes 18432 | tf_op jit(solution)/shard_map/psum | solution.py:141
  310.3 13.1 %all-reduce.3.cloned.1.call-done = f32[256,64]{0,1:T(8,128)} async-done(((f32[256,64]{0,1:T(8,128)}), f32[256,64]{0,1:T(8,128)}) %all-reduce.3.cloned.1.call-update) | async-done | bytes 65552 | tf_op jit(solution)/shard_map/psum | solution.py:141
  323.3 1.5 copy.110
  (144 shorter events, 41.0 us)
Async XLA Ops:
  7.2 41.7 %copy-start = (f32[8,64]{1,0:T(8,128)S(1)}, f32[8,64]{1,0:T(8,128)}, u32[]{:S(2)}) copy-start(f32[8,64]{1,0:T(8,128)} %param.20) | copy-start | bytes 6148
  7.2 50.9 %copy-start.11 = (s32[4]{0:T(128)S(1)}, s32[4]{0:T(128)}, u32[]{:S(2)}) copy-start(s32[4]{0:T(128)} %param.16) | copy-start | bytes 52
  7.2 66.7 %copy-start.6 = (f32[7,256]{1,0:T(8,128)S(1)}, f32[7,256]{1,0:T(8,128)}, u32[]{:S(2)}) copy-start(f32[7,256]{1,0:T(8,128)} %param.18) | copy-start | bytes 21508
  7.2 66.7 %copy-start.7 = (bf16[256,64]{0,1:T(8,128)(2,1)S(1)}, bf16[256,64]{0,1:T(8,128)(2,1)}, u32[]{:S(2)}) copy-start(bf16[256,64]{0,1:T(8,128)(2,1)} %param.19) | copy-start | bytes 98308
  10.8 63.2 %copy-start.8 = (s32[512,1]{0,1:T(1,128)}, s32[512,1]{0,1:T(1,128)S(1)}, u32[]{:S(2)}) copy-start(s32[512,1]{0,1:T(1,128)S(1)} %compare_select_fusion.1) | copy-start | bytes 6148
  14.0 15.4 %all-to-all-start = ((s32[16,128,1]{1,2,0:T(1,128)}), s32[16,128,1]{1,2,0:T(1,128)S(1)}, u32[]{:S(2)}, u32[]{:S(2)}) async-start(s32[16,128,1]{1,2,0:T(1,128)} %bitcast.22), calls=%async_computation | async-start | bytes 16384 | tf_op jit(solution)/shard_map/all_to_all | solution.py:91
  23.2 34.9 %copy-start.9 = (f32[2,64]{1,0:T(2,128)}, f32[2,64]{1,0:T(2,128)S(1)}, u32[]{:S(2)}) copy-start(f32[2,64]{1,0:T(2,128)S(1)} %convolution_maximum_fusion) | copy-start | bytes 1540
  37.4 14.6 %all-to-all-start.1 = ((f32[3,16,128]{2,0,1:T(4,128)}), f32[3,16,128]{2,0,1:T(4,128)S(1)}, u32[]{:S(2)}, u32[]{:S(2)}) async-start(f32[3,16,128]{2,0,1:T(4,128)} %copy.40), calls=%async_computation.1 | async-start | bytes 65536 | tf_op jit(solution)/shard_map/all_to_all | solution.py:97
  48.9 25.1 %copy-start.5 = (f32[2048,8]{1,0:T(8,128)}, f32[2048,8]{1,0:T(8,128)S(1)}, u32[]{:S(2)}) copy-start(f32[2048,8]{1,0:T(8,128)S(1)} %gather_fusion.3) | copy-start | bytes 196612
  50.2 0.8 copy-start.3
  51.9 20.5 %all-to-all-start.2 = ((f32[64,16,128]{2,0,1:T(8,128)}), f32[64,16,128]{2,0,1:T(8,128)S(1)}, u32[]{:S(2)}, u32[]{:S(2)}) async-start(f32[64,16,128]{2,0,1:T(8,128)} %copy_bitcast_fusion), calls=%async_computation.2 | async-start | bytes 1048576 | tf_op jit(solution)/shard_map/all_to_all | solution.py:98
  74.0 158.7 %copy-start.10 = (f32[2,64]{1,0:T(2,128)S(1)}, f32[2,64]{1,0:T(2,128)}, u32[]{:S(2)}) copy-start(f32[2,64]{1,0:T(2,128)} %copy-done.9) | copy-start | bytes 1540
  74.0 158.7 %copy-start.12 = (s32[4]{0:T(128)S(1)}, s32[4]{0:T(128)}, u32[]{:S(2)}) copy-start(s32[4]{0:T(128)} %param.16) | copy-start | bytes 52
  74.0 173.1 %copy-start.4 = (f32[64,2048]{1,0:T(8,128)S(1)}, f32[64,2048]{1,0:T(8,128)}, u32[]{:S(2)}) copy-start(f32[64,2048]{1,0:T(8,128)} %copy-done.3) | copy-start | bytes 1572868
  75.9 5.7 %copy-start.1 = (f32[64,128,256]{2,1,0:T(8,128)}, f32[64,128,256]{2,1,0:T(8,128)S(1)}, u32[]{:S(2)}) copy-start(f32[64,128,256]{2,1,0:T(8,128)S(1)} %broadcast_add_fusion.3) | copy-start | bytes 25165828 | tf_op jit(solution)/shard_map/while
  99.3 3.2 copy-start.2
  113.4 5.7 %copy-start.1 = (f32[64,128,256]{2,1,0:T(8,128)}, f32[64,128,256]{2,1,0:T(8,128)S(1)}, u32[]{:S(2)}) copy-start(f32[64,128,256]{2,1,0:T(8,128)S(1)} %broadcast_add_fusion.3) | copy-start | bytes 25165828 | tf_op jit(solution)/shard_map/while
  136.8 3.2 copy-start.2
  150.9 5.7 %copy-start.1 = (f32[64,128,256]{2,1,0:T(8,128)}, f32[64,128,256]{2,1,0:T(8,128)S(1)}, u32[]{:S(2)}) copy-start(f32[64,128,256]{2,1,0:T(8,128)S(1)} %broadcast_add_fusion.3) | copy-start | bytes 25165828 | tf_op jit(solution)/shard_map/while
  174.3 3.2 copy-start.2
  188.4 5.7 %copy-start.1 = (f32[64,128,256]{2,1,0:T(8,128)}, f32[64,128,256]{2,1,0:T(8,128)S(1)}, u32[]{:S(2)}) copy-start(f32[64,128,256]{2,1,0:T(8,128)S(1)} %broadcast_add_fusion.3) | copy-start | bytes 25165828 | tf_op jit(solution)/shard_map/while
  211.8 3.2 copy-start.2
  228.5 18.6 %all-to-all-start.3 = ((f32[64,16,128]{2,0,1:T(8,128)}), f32[64,16,128]{2,0,1:T(8,128)S(1)}, u32[]{:S(2)}, u32[]{:S(2)}) async-start(f32[64,16,128]{2,0,1:T(8,128)} %copy.51), calls=%async_computation.3 | async-start | bytes 1048576 | tf_op jit(solution)/shard_map/all_to_all | solution.py:134
  232.6 90.8 %all-reduce.3.cloned.1.call-start = ((), (), s32[]{:S(2)}) async-start(), calls=%async_computation.4 | async-start | bytes 131072 | tf_op jit(solution)/shard_map/psum | solution.py:141
Sparse Core Ops, SparseCore 0:
  237.4 85.8 all-reduce.2
where the time goes:
time: 334 us; the launch traced here: 332 us
  matrix products  76.2 us (23%)
  other arithmetic  60.9 us (18%)
  blocking collectives  60.2 us (18%)
  local copies, waits for them, and re-layouts  60.1 us (18%)
  waiting for transfers between devices  35.7 us (11%)
  starting transfers between devices  23.5 us (7%)
  between operations  14.4 us (4%)
    psum x1, blocking collectives, per_device(): lax.psum((jnp.sum(dfirst, axis=0), jnp.sum(dsecond, axis=0), lift_part),...  60.2 us
    dot_general x4, matrix products, pair_terms(): lax.dot_general(dkernel, w_second, (((0,), (1,)), ((), ())), preferred_el...  45.2 us
    tanh x4, other arithmetic, pair_terms(): activ, slope_fn = jax.vjp(jax.nn.gelu, preact)  22.9 us
    dot_general x4, matrix products, pair_terms(): lax.dot_general(hidden, dkernel, (((0,), (1,)), ((), ())), preferred_elem...  15.7 us
    reduce_sum x4, other arithmetic, pair_terms(): per_point = jnp.sum(dpre, axis=0)  15.7 us
    while x20, local copies, waits for them, and re-layouts  14.4 us
    psum x1, waiting for transfers between devices, per_device(): lax.psum((jnp.sum(dfirst, axis=0), jnp.sum(dsecond, axis=0), lift_part),...  13.1 us
    all_to_all x1, waiting for transfers between devices, per_device(): lax.all_to_all(sent_feat, 'slab', split_axis=1, concat_axis=1, tiled=True)  11.7 us
  transfers between devices with their start and end apart: 5, of which 3 were waited for; matrix products, arithmetic and copies ran while one was open for 7% of the time, Pallas kernels for 0%

commit v1 on v0

v1 whole, which is shorter than its diff:
```python
import functools

import jax
import jax.numpy as jnp
from jax import lax
from jax.experimental import pallas as pl
from jax.experimental.pallas import tpu as pltpu
from jax.sharding import PartitionSpec as P

BLOCK_PTS = 128
BLOCK_CELLS = 64
GRID_ROW = 16
GROUP = 8
CHUNK = 64
GELU_A = 0.7978845608028654
GELU_B = 0.044715 * GELU_A

PREC = lax.Precision.HIGHEST
F32 = jnp.float32
BF16 = jnp.bfloat16


def nn(a, b):
    return lax.dot_general(a, b, (((1,), (0,)), ((), ())), preferred_element_type=F32)


def nt(a, b, precision=None):
    return lax.dot_general(
        a, b, (((1,), (1,)), ((), ())), precision=precision, preferred_element_type=F32
    )


def tn_exact(a, b):
    return lax.dot_general(
        a, b, (((0,), (0,)), ((), ())), precision=PREC, preferred_element_type=F32
    )


def halves(value):
    high = value.astype(BF16)
    return high, (value - high.astype(F32)).astype(BF16)


def iota(shape, axis):
    return lax.broadcasted_iota(jnp.int32, shape, axis)


def body(
    peers,
    pos_ref,
    input_ref,
    owner_ref,
    local_ref,
    pair_ref,
    mask_ref,
    first_ref,
    second_ref,
    lift_ref,
    cot_ref,
    latent_ref,
    gfirst_ref,
    gsecond_ref,
    glift_ref,
    place_ref,
    want_out,
    want_in,
    table_ref,
    reply_out,
    reply_in,
    cellpart_ref,
    gcell_ref,
    cellrow_ref,
    pointpart_ref,
    feat_ref,
    yrow_ref,
    dk_ref,
    dh_ref,
    hid_ref,
    dpre_ref,
    lat_ref,
    dfeat_ref,
    dsec_ref,
    dfir_ref,
    flat_ref,
    part_out,
    part_in,
    total_out,
    total_in,
    want_send,
    want_recv,
    reply_send,
    reply_recv,
    part_send,
    part_recv,
    total_send,
    total_recv,
):
    me = lax.axis_index("slab")
    req_count = local_ref.shape[1]
    capacity = want_in.shape[2]
    pairs = mask_ref.shape[0]
    cells = cot_ref.shape[1]
    blocks = cells // BLOCK_CELLS
    groups = BLOCK_CELLS // GROUP
    channels = cot_ref.shape[0]
    width = first_ref.shape[1]
    share = part_in.shape[1]

    barrier = pltpu.get_barrier_semaphore()

    def greet(step, carry):
        peer = lax.rem(me + step, peers)
        pl.semaphore_signal(barrier, inc=1, device_id={"slab": peer})
        return carry

    lax.fori_loop(1, peers, greet, 0)

    def exchange(source, target, send, recv, step):
        peer = lax.rem(me + step, peers)
        return pltpu.make_async_remote_copy(
            src_ref=source.at[peer],
            dst_ref=target.at[me],
            send_sem=send.at[peer],
            recv_sem=recv.at[me],
            device_id={"slab": peer},
        )

    def arrival(target, send, recv, step):
        peer = lax.rem(me + step, peers)
        return peer, pltpu.make_async_remote_copy(
            src_ref=target.at[peer],
            dst_ref=target.at[peer],
            send_sem=send.at[peer],
            recv_sem=recv.at[peer],
            device_id={"slab": peer},
        )

    owner = owner_ref[...]
    local = local_ref[...]
    named = jnp.where(owner == iota((peers, req_count), 0), 1.0, 0.0)
    earlier = jnp.where(
        iota((req_count, req_count), 0) < iota((req_count, req_count), 1), 1.0, 0.0
    ).astype(BF16)
    rank = jnp.sum(named * nn(named.astype(BF16), earlier), axis=0, keepdims=True)
    slot = owner * capacity + rank.astype(jnp.int32)
    line = iota((16, req_count), 0)
    digits = jnp.where(
        line == 0, local >> 7, jnp.where(line == 1, local & 127, 0)
    ).astype(F32).astype(BF16)
    for p in range(peers):
        place = jnp.where(
            slot == p * capacity + iota((capacity, req_count), 0), 1.0, 0.0
        ).astype(BF16)
        place_ref[p] = place
        found = nt(digits, place)
        want_out[p] = (found[0:1] * 128.0 + found[1:2]).astype(jnp.int32)

    pl.semaphore_wait(barrier, peers - 1)

    def ask(step, carry):
        exchange(want_out, want_in, want_send, want_recv, step).start()
        return carry

    lax.fori_loop(1, peers, ask, 0)
    want_in[me] = want_out[me]

    highs = input_ref.shape[1] // 128
    for h in range(highs):
        lanes = slice(h * 128, (h + 1) * 128)
        upper, lower = halves(input_ref[:, lanes])
        table_ref[h * 16 : h * 16 + 8, 0:128] = upper
        table_ref[h * 16 : h * 16 + 8, 128:256] = lower
        coords = jnp.concatenate([pos_ref[:, lanes], jnp.zeros((5, 128), F32)], axis=0)
        upper, lower = halves(coords)
        table_ref[h * 16 + 8 : h * 16 + 16, 0:128] = upper
        table_ref[h * 16 + 8 : h * 16 + 16, 128:256] = lower

    def provide(peer):
        wanted = want_in[peer]
        one = jnp.where((wanted & 127) == iota((128, capacity), 0), 1.0, 0.0).astype(BF16)
        rows = nn(table_ref[...], jnp.concatenate([one, one], axis=0))
        rows = rows.reshape(highs, 16, capacity)
        chosen = (wanted >> 7) == iota((highs, 1, capacity), 0)
        rows = jnp.sum(jnp.where(chosen, rows, 0.0), axis=0)
        reply_out[peer] = rows[0 : reply_out.shape[1]]

    provide(me)

    def answer(step, carry):
        peer, got = arrival(want_in, want_send, want_recv, peers - step)
        got.wait_recv()
        provide(peer)
        exchange(reply_out, reply_in, reply_send, reply_recv, peers - step).start()
        return carry

    lax.fori_loop(1, peers, answer, 0)
    reply_in[me] = reply_out[me]

    counts = []
    ones = jnp.ones((16, BLOCK_PTS), BF16)
    per_pair = [nt(ones, mask_ref[j].astype(F32).astype(BF16))[0:1] for j in range(pairs)]
    for b in range(blocks):
        count = jnp.zeros((1, BLOCK_CELLS), F32)
        for j in range(pairs):
            count = count + jnp.where(pair_ref[j] == b, per_pair[j], 0.0)
        counts.append(count)
    divisor = jnp.maximum(jnp.concatenate(counts, axis=1), 1.0)
    gcells = cot_ref[...] / divisor
    index = iota((16, cells), 1)
    column = (lax.rem(index, GRID_ROW).astype(F32) + 0.5) / GRID_ROW
    row = (lax.div(index, GRID_ROW).astype(F32) + 0.5) * GRID_ROW / cells
    third = (me.astype(F32) + 0.5) / peers
    line = iota((16, cells), 0)
    coords = jnp.where(line == 0, column, jnp.where(line == 1, row, third))
    shifted = jnp.where(
        line == 3,
        column,
        jnp.where(
            line == 4, row, jnp.where(line == 5, third, jnp.where(line == 6, 1.0, 0.0))
        ),
    )
    first = first_ref[...]
    cell_weights = jnp.concatenate([first[3:7], jnp.zeros((4, width), F32)], axis=0)
    cell_values = jnp.where(line == 3, 1.0, jnp.where(line < 3, coords, 0.0))[0:8]
    cellpart = tn_exact(cell_weights, cell_values)
    for k in range(blocks * groups):
        turn = (cells - k * GROUP) % cells
        for value, into in ((cellpart, cellpart_ref), (gcells, gcell_ref), (shifted, cellrow_ref)):
            into[k] = pltpu.roll(value, turn, 1) if turn else value
    half_second = (second_ref[...].astype(F32) * 0.5)
    half_turned = half_second.T.astype(BF16)
    half_second = half_second.astype(BF16)
    lat_ref[...] = jnp.zeros_like(lat_ref)
    dsec_ref[...] = jnp.zeros_like(dsec_ref)
    dfir_ref[...] = jnp.zeros_like(dfir_ref)
    dfeat_ref[...] = jnp.zeros_like(dfeat_ref)

    def settle(step, carry):
        peer, got = arrival(reply_in, reply_send, reply_recv, step)
        got.wait()
        _, sent = arrival(want_in, want_send, want_recv, step)
        sent.wait_send()
        return carry

    lax.fori_loop(1, peers, settle, 0)
    read = jnp.zeros((reply_in.shape[1], req_count), F32)
    for p in range(peers):
        upper, lower = halves(reply_in[p])
        read = read + (nn(upper, place_ref[p]) + nn(lower, place_ref[p]))
    inputs = read[0:8]
    points = jnp.concatenate([read[8:11], jnp.zeros((5, req_count), F32)], axis=0)
    req_z = tn_exact(lift_ref[...], inputs)
    gate = jax.nn.sigmoid(req_z)
    feats = req_z * gate
    slope = gate * (1.0 + req_z * (1.0 - gate))
    point_weights = jnp.concatenate([first[0:3], jnp.zeros((5, width), F32)], axis=0)
    pointpart = tn_exact(point_weights, points)
    upper = points.astype(BF16).astype(F32)
    both = jnp.concatenate([upper, points - upper], axis=0)
    for j in range(pairs):
        lanes = slice(j * BLOCK_PTS, (j + 1) * BLOCK_PTS)
        feat_ref[j] = feats[:, lanes]
        pointpart_ref[j] = pointpart[:, lanes]
        yrow_ref[j] = both[:, lanes]

    def work(step, carry):
        j = step // groups
        i = step % groups
        cell_block = pair_ref[j]
        at = cell_block * groups + i
        mask = mask_ref[j, pl.ds(pl.multiple_of(i * GROUP, GROUP), GROUP), :].astype(F32)
        feat = feat_ref[j]
        grads = gcell_ref[at]
        for s in range(GROUP):
            lanes = slice(s * BLOCK_PTS, (s + 1) * BLOCK_PTS)
            dk_ref[:, lanes] = ((feat * mask[s : s + 1]) * grads[:, s : s + 1]).astype(BF16)
        for s in range(0, GROUP, 2):
            lanes = slice(s * BLOCK_PTS, (s + 2) * BLOCK_PTS)
            dh_ref[:, lanes] = nn(half_second, dk_ref[:, lanes])
        for s in range(GROUP):
            lanes = slice(s * BLOCK_PTS, (s + 1) * BLOCK_PTS)
            for h in range(0, width, CHUNK):
                rows = slice(h, h + CHUNK)
                x = pointpart_ref[j, rows, :] + cellpart_ref[at, rows, s : s + 1]
                square = x * x
                t = jnp.tanh(x * (GELU_A + GELU_B * square))
                u = 1.0 + t
                hid = x * u
                hid_ref[rows, lanes] = hid.astype(BF16)
                bend = hid * (1.0 - t) * (GELU_A + (3.0 * GELU_B) * square)
                dpre_ref[rows, lanes] = ((u + bend) * dh_ref[rows, lanes]).astype(BF16)
        lat = jnp.zeros((channels, cells), F32)
        dfeat = jnp.zeros((channels, BLOCK_PTS), F32)
        lane = iota((channels, cells), 1)
        sides = []
        for s in range(0, GROUP, 2):
            pair_lanes = slice(s * BLOCK_PTS, (s + 2) * BLOCK_PTS)
            kernels = nn(half_turned, hid_ref[:, pair_lanes])
            for d in range(2):
                c = s + d
                masked = kernels[:, d * BLOCK_PTS : (d + 1) * BLOCK_PTS] * mask[c : c + 1]
                total = jnp.sum(masked * feat, axis=1, keepdims=True)
                lat = lat + jnp.where(
                    lane == cell_block * BLOCK_CELLS + i * GROUP + c, total, 0.0
                )
                dfeat = dfeat + masked * grads[:, c : c + 1]
                sides.append((yrow_ref[j] + cellrow_ref[at][:, c : c + 1]).astype(BF16))
        lat_ref[...] += lat
        dfeat_ref[j] += dfeat
        dsec_ref[...] += nt(dk_ref[...], hid_ref[...])
        dfir_ref[...] += nt(jnp.concatenate(sides, axis=1), dpre_ref[...])
        return carry

    lax.fori_loop(0, pairs * groups, work, 0)

    latent_ref[...] = (lat_ref[...] / divisor).astype(BF16)
    dfeat = jnp.concatenate([dfeat_ref[j] for j in range(pairs)], axis=1)
    lift = nt(inputs, dfeat * slope, PREC)
    half = width // 2
    flat_ref[...] = jnp.zeros_like(flat_ref)
    dsec = dsec_ref[...] * 0.5
    dfir = dfir_ref[0:8] + dfir_ref[8:16]
    flat_ref[0:channels] = dsec[:, :half]
    flat_ref[channels : 2 * channels] = dsec[:, half:]
    flat_ref[2 * channels : 2 * channels + 8] = dfir[:, :half]
    flat_ref[2 * channels + 8 : 2 * channels + 16] = dfir[:, half:]
    flat_ref[2 * channels + 16 : 2 * channels + 24, 0:channels] = lift
    for p in range(peers):
        part_out[p] = flat_ref[p * share : (p + 1) * share]

    def scatter(step, carry):
        exchange(part_out, part_in, part_send, part_recv, step).start()
        return carry

    lax.fori_loop(1, peers, scatter, 0)
    part_in[me] = part_out[me]

    def take(step, carry):
        _, got = arrival(part_in, part_send, part_recv, step)
        got.wait()
        return carry

    lax.fori_loop(1, peers, take, 0)
    total_out[...] = jnp.sum(part_in[...], axis=0)

    def spread(step):
        peer = lax.rem(me + step, peers)
        return pltpu.make_async_remote_copy(
            src_ref=total_out,
            dst_ref=total_in.at[me],
            send_sem=total_send.at[peer],
            recv_sem=total_recv.at[me],
            device_id={"slab": peer},
        )

    def give(step, carry):
        spread(step).start()
        return carry

    lax.fori_loop(1, peers, give, 0)
    total_in[me] = total_out[...]

    def collect(step, carry):
        _, got = arrival(total_in, total_send, total_recv, step)
        got.wait()
        return carry

    lax.fori_loop(1, peers, collect, 0)
    for p in range(peers):
        flat_ref[p * share : (p + 1) * share] = total_in[p]
    gsecond_ref[0:half] = flat_ref[0:channels].T
    gsecond_ref[half:width] = flat_ref[channels : 2 * channels].T
    gfirst_ref[:, 0:half] = flat_ref[2 * channels : 2 * channels + 7]
    gfirst_ref[:, half:width] = flat_ref[2 * channels + 8 : 2 * channels + 15]
    glift_ref[...] = flat_ref[2 * channels + 16 : 2 * channels + 24, 0:channels]


def per_device(
    point_pos,
    point_input,
    req_owner,
    req_local,
    pair_cell,
    pair_mask,
    w_first,
    w_second,
    w_lift,
    cotangent,
):
    peers = lax.axis_size("slab")
    req_count = req_local.shape[0]
    capacity = 4 * req_count // peers
    channels, cells = cotangent.shape
    width = w_first.shape[1]
    pairs = pair_mask.shape[0]
    points = point_input.shape[1]
    rows = point_input.shape[0] + point_pos.shape[0]
    kinds = cells // GROUP
    share = -(-(2 * channels + 24) // peers)
    span = GROUP * BLOCK_PTS
    vmem = pl.BlockSpec(memory_space=pltpu.VMEM)
    sems = [pltpu.SemaphoreType.DMA((peers,))] * 8
    return pl.pallas_call(
        functools.partial(body, peers),
        out_shape=(
            jax.ShapeDtypeStruct((channels, cells), BF16),
            jax.ShapeDtypeStruct(w_first.shape, F32),
            jax.ShapeDtypeStruct(w_second.shape, F32),
            jax.ShapeDtypeStruct(w_lift.shape, F32),
        ),
        in_specs=[vmem] * 4 + [pl.BlockSpec(memory_space=pltpu.SMEM)] + [vmem] * 5,
        out_specs=[vmem] * 4,
        scratch_shapes=[
            pltpu.VMEM((peers, capacity, req_count), BF16),
            pltpu.VMEM((peers, 1, capacity), jnp.int32),
            pltpu.VMEM((peers, 1, capacity), jnp.int32),
            pltpu.VMEM((points // 128 * 16, 256), BF16),
            pltpu.VMEM((peers, rows, capacity), F32),
            pltpu.VMEM((peers, rows, capacity), F32),
            pltpu.VMEM((kinds, width, cells), F32),
            pltpu.VMEM((kinds, channels, cells), F32),
            pltpu.VMEM((kinds, 16, cells), F32),
            pltpu.VMEM((pairs, width, BLOCK_PTS), F32),
            pltpu.VMEM((pairs, channels, BLOCK_PTS), F32),
            pltpu.VMEM((pairs, 16, BLOCK_PTS), F32),
            pltpu.VMEM((channels, span), BF16),
            pltpu.VMEM((width, span), F32),
            pltpu.VMEM((width, span), BF16),
            pltpu.VMEM((width, span), BF16),
            pltpu.VMEM((channels, cells), F32),
            pltpu.VMEM((pairs, channels, BLOCK_PTS), F32),
            pltpu.VMEM((channels, width), F32),
            pltpu.VMEM((16, width), F32),
            pltpu.VMEM((peers * share, 128), F32),
            pltpu.VMEM((peers, share, 128), F32),
            pltpu.VMEM((peers, share, 128), F32),
            pltpu.VMEM((share, 128), F32),
            pltpu.VMEM((peers, share, 128), F32),
        ]
        + sems,
        compiler_params=pltpu.CompilerParams(
            collective_id=0, has_side_effects=True, vmem_limit_bytes=40 * 1024 * 1024
        ),
    )(
        point_pos,
        point_input,
        req_owner.reshape(1, req_count),
        req_local.reshape(1, req_count),
        pair_cell,
        pair_mask,
        w_first,
        w_second,
        w_lift,
        cotangent,
    )


def solution(mesh):
    split = ("groups", "slab")
    in_specs = (
        P(None, split),
        P(None, split),
        P(split, None),
        P(split),
        P(split),
        P(split, None, None),
        P(),
        P(),
        P(),
        P(None, split),
    )
    out_specs = (P(None, split), P("groups", None), P("groups", None), P("groups", None))
    return jax.shard_map(
        per_device, mesh=mesh, in_specs=in_specs, out_specs=out_specs, check_vma=False
    )
```

time: 334 us -> 76.1 us (0.23)
  matrix products: 76.2 us -> 0 us
  Pallas kernels: 0 us -> 67.8 us
  other arithmetic: 60.9 us -> 0 us
  blocking collectives: 60.2 us -> 0 us
  local copies, waits for them, and re-layouts: 60.1 us -> 7.3 us
  waiting for transfers between devices: 35.7 us -> 0 us
  starting transfers between devices: 23.5 us -> 0 us
  between operations: 14.4 us -> 0.72 us
    dot_general x32 -> x0, matrix products: 76.2 us -> none  [the longest x4 45.2 us: pair_terms(): lax.dot_general(dkernel, w_second, (((0,), (1,)), ((), ())), preferred_el...]
    pallas_call x0 -> x1, Pallas kernels: none -> 67.8 us  [per_device(): pl.pallas_call(functools.partial(body, peers), out_shape=(jax.ShapeDtypeS...]
    psum x1 -> x0, blocking collectives: 60.2 us -> none  [per_device(): lax.psum((jnp.sum(dfirst, axis=0), jnp.sum(dsecond, axis=0), lift_part),...]
    reduce_sum x16 -> x0, other arithmetic: 29.2 us -> none  [the longest x4 15.7 us: pair_terms(): per_point = jnp.sum(dpre, axis=0)]
    all_to_all x4 -> x0, starting transfers between devices: 23.5 us -> none  [the longest x1 7.39 us: per_device(): lax.all_to_all(wanted, 'slab', split_axis=0, concat_axis=0, tiled=True)]
    tanh x4 -> x0, other arithmetic: 22.9 us -> none  [pair_terms(): activ, slope_fn = jax.vjp(jax.nn.gelu, preact)]
    all_to_all x4 -> x0, waiting for transfers between devices: 22.6 us -> none  [the longest x1 11.7 us: per_device(): lax.all_to_all(sent_feat, 'slab', split_axis=1, concat_axis=1, tiled=True)]
    gather x6 -> x0, local copies, waits for them, and re-layouts: 15.7 us -> none  [the longest x1 7.05 us: per_device(): sent_pos = point_pos[:, asked]]
  transfers between devices with their start and end apart: 5 -> 0, of which waited for: 3 -> 0; matrix products, arithmetic and copies ran while one was open for 7% -> 0% of each run, Pallas kernels for 0% -> 0%
where the time goes in v1:
time: 76.1 us; the launch traced here: 75.8 us
  Pallas kernels  67.8 us (89%)
  local copies, waits for them, and re-layouts  7.3 us (10%)
    pallas_call x1, Pallas kernels, per_device(): pl.pallas_call(functools.partial(body, peers), out_shape=(jax.ShapeDtypeS...  67.8 us
    unnamed x22, local copies, waits for them, and re-layouts  6.59 us

profile of v1, /device:TPU:0, one launch (start us, length us, event | category | flops | bytes accessed | tf_op | source)
XLA Modules:
  0.0 75.8 jit_solution(17167220592940140436)
XLA Ops:
  0.6 0.0 copy-start.2
  0.6 0.0 copy-start.3
  0.7 0.0 copy-start.6
  0.7 0.0 copy-start.8
  0.7 0.9 %copy.14.second_ref = bf16[256,64]{1,0:T(8,128)(2,1)S(1)} copy(bf16[256,64]{0,1:T(8,128)(2,1)} %param.17) | data formatting | bytes 65536 | tf_op args[7]
  1.6 0.0 copy-done.2
  1.6 0.0 copy-done.3
  1.6 0.0 copy-done.6
  1.6 0.0 copy-done.8
  1.6 0.0 copy-start
  1.6 0.9 %copy-done = f32[8,4096]{1,0:T(8,128)S(1)} copy-done((f32[8,4096]{1,0:T(8,128)S(1)}, f32[8,4096]{1,0:T(8,128)}, u32[]{:S(2)}) %copy-start) | copy-done | bytes 131096
  2.5 0.0 copy-start.1
  2.5 0.9 %copy-done.1 = s32[4,64,128]{2,1,0:T(8,128)S(1)} copy-done((s32[4,64,128]{2,1,0:T(8,128)S(1)}, s32[4,64,128]{2,1,0:T(8,128)}, u32[]{:S(2)}) %copy-start.1) | copy-done | bytes 131096
  3.4 0.0 copy-start.4
  3.4 0.7 copy-done.4
  4.1 0.0 copy-start.5
  4.1 0.7 copy-done.5
  4.8 0.0 copy-start.7
  4.8 0.7 copy-done.7
  5.5 67.8 %shard_map.129 = (bf16[64,128]{1,0:T(8,128)(2,1)S(1)}, f32[7,256]{1,0:T(8,128)S(1)}, f32[256,64]{1,0:T(8,128)S(1)}, f32[8,64]{1,0:T(8,128)S(1)}) custom-call(f32[3,4096]{1,0:T(4,128)S(1)} %copy-done.2, f32[8,4096]{1,0:T(8,128)S(1)} %copy-done, s32[1,512]{1,0:T(1,128)S(1)} %bitcast.2, s32[1,512]{1,0:T(1,128)S(1)} %bitcast.3, s32[4]{0:T(128)S(1)} %copy-done.8, ...), custom_call_target="tpu_custom_call" | custom-call | tf_op jit(solution)/shard_map/pallas_call | solution.py:403
  73.3 0.7 copy.15
  74.0 0.6 copy.19
  74.6 0.6 copy.20
  75.2 0.6 copy.21
Async XLA Ops:
  0.6 1.0 %copy-start.2 = (f32[3,4096]{1,0:T(4,128)S(1)}, f32[3,4096]{1,0:T(4,128)}, u32[]{:S(2)}) copy-start(f32[3,4096]{1,0:T(4,128)} %pos_ref.1) | copy-start | bytes 147460
  0.6 1.0 %copy-start.3 = (f32[64,128]{1,0:T(8,128)S(1)}, f32[64,128]{1,0:T(8,128)}, u32[]{:S(2)}) copy-start(f32[64,128]{1,0:T(8,128)} %cot_ref.1) | copy-start | bytes 98308
  0.7 1.0 %copy-start.6 = (s32[512,1]{0,1:T(1,128)S(1)}, s32[512,1]{0,1:T(1,128)}, u32[]{:S(2)}) copy-start(s32[512,1]{0,1:T(1,128)} %param.12) | copy-start | bytes 6148
  0.7 1.0 %copy-start.8 = (s32[4]{0:T(128)S(1)}, s32[4]{0:T(128)}, u32[]{:S(2)}) copy-start(s32[4]{0:T(128)} %pair_ref.1) | copy-start | bytes 52
  1.6 0.9 %copy-start = (f32[8,4096]{1,0:T(8,128)S(1)}, f32[8,4096]{1,0:T(8,128)}, u32[]{:S(2)}) copy-start(f32[8,4096]{1,0:T(8,128)} %input_ref.1) | copy-start | bytes 393220
  2.5 0.9 %copy-start.1 = (s32[4,64,128]{2,1,0:T(8,128)S(1)}, s32[4,64,128]{2,1,0:T(8,128)}, u32[]{:S(2)}) copy-start(s32[4,64,128]{2,1,0:T(8,128)} %mask_ref.1) | copy-start | bytes 393220
  3.4 0.7 copy-start.4
  4.1 0.7 copy-start.5
  4.8 0.7 copy-start.7

commit v2 on v1

--- a/solution.py
+++ b/solution.py
@@ -1,5 +1,7 @@
 import functools
 
+import ml_dtypes
+import numpy as np
 import jax
 import jax.numpy as jnp
 from jax import lax
@@ -15,6 +17,10 @@
 GELU_A = 0.7978845608028654
 GELU_B = 0.044715 * GELU_A
 
+ONE = np.array(1.0, ml_dtypes.bfloat16)
+A16 = np.array(GELU_A, ml_dtypes.bfloat16)
+B16 = np.array(GELU_B, ml_dtypes.bfloat16)
+C16 = np.array(3.0*GELU_B, ml_dtypes.bfloat16)
 PREC = lax.Precision.HIGHEST
 F32 = jnp.float32
 BF16 = jnp.bfloat16
@@ -77,6 +83,8 @@
     dh_ref,
     hid_ref,
     dpre_ref,
+    side_ref,
+    wpre_ref,
     lat_ref,
     dfeat_ref,
     dsec_ref,
@@ -108,29 +116,36 @@
 
     barrier = pltpu.get_barrier_semaphore()
 
+    def loop(act):
+        lax.fori_loop(1, peers, act, 0, unroll=1)
+
     def greet(step, carry):
         peer = lax.rem(me + step, peers)
         pl.semaphore_signal(barrier, inc=1, device_id={"slab": peer})
         return carry
 
-    lax.fori_loop(1, peers, greet, 0)
+    loop(greet)
 
     def exchange(source, target, send, recv, step):
         peer = lax.rem(me + step, peers)
         return pltpu.make_async_remote_copy(
             src_ref=source.at[peer],
             dst_ref=target.at[me],
-            send_sem=send.at[peer],
-            recv_sem=recv.at[me],
+            send_sem=send,
+            recv_sem=recv.at[me] if recv is want_recv else recv,
             device_id={"slab": peer},
         )
+
+    def drain(like, sem):
+        part = like.at[pl.ds(0, peers - 1)]
+        pltpu.make_async_copy(part, part, sem).wait()
 
     def arrival(target, send, recv, step):
         peer = lax.rem(me + step, peers)
         return peer, pltpu.make_async_remote_copy(
             src_ref=target.at[peer],
             dst_ref=target.at[peer],
-            send_sem=send.at[peer],
+            send_sem=send,
             recv_sem=recv.at[peer],
             device_id={"slab": peer},
         )
@@ -161,7 +176,7 @@
         exchange(want_out, want_in, want_send, want_recv, step).start()
         return carry
 
-    lax.fori_loop(1, peers, ask, 0)
+    loop(ask)
     want_in[me] = want_out[me]
 
     highs = input_ref.shape[1] // 128
@@ -193,7 +208,7 @@
         exchange(reply_out, reply_in, reply_send, reply_recv, peers - step).start()
         return carry
 
-    lax.fori_loop(1, peers, answer, 0)
+    loop(answer)
     reply_in[me] = reply_out[me]
 
     counts = []
@@ -227,22 +242,26 @@
         turn = (cells - k * GROUP) % cells
         for value, into in ((cellpart, cellpart_ref), (gcells, gcell_ref), (shifted, cellrow_ref)):
             into[k] = pltpu.roll(value, turn, 1) if turn else value
-    half_second = (second_ref[...].astype(F32) * 0.5)
-    half_turned = half_second.T.astype(BF16)
-    half_second = half_second.astype(BF16)
+    half_turned = second_ref[...].astype(F32) * 0.5
+    half_second = half_turned.T.astype(BF16)
+    half_turned = half_turned.astype(BF16)
+    eight = jnp.concatenate([first, jnp.zeros((1, width), F32)], axis=0)
+    coarse = eight.astype(BF16).astype(F32)
+    wpre_ref[...] = jnp.concatenate(
+        [
+            coarse,
+            jnp.where(iota((8, width), 0) < 3, coarse, 0.0),
+            eight - coarse,
+            jnp.zeros((8, width), F32),
+        ],
+        axis=0,
+    ).T.astype(BF16)
     lat_ref[...] = jnp.zeros_like(lat_ref)
     dsec_ref[...] = jnp.zeros_like(dsec_ref)
     dfir_ref[...] = jnp.zeros_like(dfir_ref)
     dfeat_ref[...] = jnp.zeros_like(dfeat_ref)
 
-    def settle(step, carry):
-        peer, got = arrival(reply_in, reply_send, reply_recv, step)
-        got.wait()
-        _, sent = arrival(want_in, want_send, want_recv, step)
-        sent.wait_send()
-        return carry
-
-    lax.fori_loop(1, peers, settle, 0)
+    drain(reply_in, reply_recv)
     read = jnp.zeros((reply_in.shape[1], req_count), F32)
     for p in range(peers):
         upper, lower = halves(reply_in[p])
@@ -271,31 +290,34 @@
         mask = mask_ref[j, pl.ds(pl.multiple_of(i * GROUP, GROUP), GROUP), :].astype(F32)
         feat = feat_ref[j]
         grads = gcell_ref[at]
-        for s in range(GROUP):
-            lanes = slice(s * BLOCK_PTS, (s + 1) * BLOCK_PTS)
-            dk_ref[:, lanes] = ((feat * mask[s : s + 1]) * grads[:, s : s + 1]).astype(BF16)
-        for s in range(0, GROUP, 2):
-            lanes = slice(s * BLOCK_PTS, (s + 2) * BLOCK_PTS)
-            dh_ref[:, lanes] = nn(half_second, dk_ref[:, lanes])
-        for s in range(GROUP):
-            lanes = slice(s * BLOCK_PTS, (s + 1) * BLOCK_PTS)
+        lane = iota((channels, cells), 1)
+        rows_now = cellrow_ref[at]
+        yrow = yrow_ref[j]
+
+        def forward(s):
+            both_lanes = slice(s * BLOCK_PTS, (s + 2) * BLOCK_PTS)
+            for c in (s, s + 1):
+                lanes = slice(c * BLOCK_PTS, (c + 1) * BLOCK_PTS)
+                dk_ref[:, lanes] = ((feat * mask[c : c + 1]) * grads[:, c : c + 1]).astype(BF16)
+                side = (yrow + rows_now[:, c : c + 1]).astype(BF16)
+                side_ref[0:16, lanes] = side
+                side_ref[16:32, lanes] = side
+            dh_ref[:, both_lanes] = nn(half_second, dk_ref[:, both_lanes])
+            pre = nn(wpre_ref[...], side_ref[:, both_lanes])
             for h in range(0, width, CHUNK):
                 rows = slice(h, h + CHUNK)
-                x = pointpart_ref[j, rows, :] + cellpart_ref[at, rows, s : s + 1]
+                x = pre[rows].astype(BF16)
                 square = x * x
-                t = jnp.tanh(x * (GELU_A + GELU_B * square))
-                u = 1.0 + t
+                t = jnp.tanh(x * (A16 + B16 * square))
+                u = ONE + t
                 hid = x * u
-                hid_ref[rows, lanes] = hid.astype(BF16)
-                bend = hid * (1.0 - t) * (GELU_A + (3.0 * GELU_B) * square)
-                dpre_ref[rows, lanes] = ((u + bend) * dh_ref[rows, lanes]).astype(BF16)
-        lat = jnp.zeros((channels, cells), F32)
-        dfeat = jnp.zeros((channels, BLOCK_PTS), F32)
-        lane = iota((channels, cells), 1)
-        sides = []
-        for s in range(0, GROUP, 2):
-            pair_lanes = slice(s * BLOCK_PTS, (s + 2) * BLOCK_PTS)
-            kernels = nn(half_turned, hid_ref[:, pair_lanes])
+                hid_ref[rows, both_lanes] = hid
+                bend = hid * (ONE - t) * (A16 + C16 * square)
+                dpre_ref[rows, both_lanes] = (u + bend) * dh_ref[rows, both_lanes].astype(BF16)
+
+        def backward(s, lat, dfeat):
+            both_lanes = slice(s * BLOCK_PTS, (s + 2) * BLOCK_PTS)
+            kernels = nn(half_turned, hid_ref[:, both_lanes])
             for d in range(2):
                 c = s + d
                 masked = kernels[:, d * BLOCK_PTS : (d + 1) * BLOCK_PTS] * mask[c : c + 1]
@@ -304,11 +326,19 @@
                     lane == cell_block * BLOCK_CELLS + i * GROUP + c, total, 0.0
                 )
                 dfeat = dfeat + masked * grads[:, c : c + 1]
-                sides.append((yrow_ref[j] + cellrow_ref[at][:, c : c + 1]).astype(BF16))
+            return lat, dfeat
+
+        lat = jnp.zeros((channels, cells), F32)
+        dfeat = jnp.zeros((channels, BLOCK_PTS), F32)
+        for s in range(0, GROUP, 2):
+            forward(s)
+            if s:
+                lat, dfeat = backward(s - 2, lat, dfeat)
+        lat, dfeat = backward(GROUP - 2, lat, dfeat)
         lat_ref[...] += lat
         dfeat_ref[j] += dfeat
-        dsec_ref[...] += nt(dk_ref[...], hid_ref[...])
-        dfir_ref[...] += nt(jnp.concatenate(sides, axis=1), dpre_ref[...])
+        dsec_ref[...] += nt(hid_ref[...], dk_ref[...])
+        dfir_ref[...] += nt(side_ref[0:16], dpre_ref[...])
         return carry
 
     lax.fori_loop(0, pairs * groups, work, 0)
@@ -318,7 +348,7 @@
     lift = nt(inputs, dfeat * slope, PREC)
     half = width // 2
     flat_ref[...] = jnp.zeros_like(flat_ref)
-    dsec = dsec_ref[...] * 0.5
+    dsec = dsec_ref[...].T * 0.5
     dfir = dfir_ref[0:8] + dfir_ref[8:16]
     flat_ref[0:channels] = dsec[:, :half]
     flat_ref[channels : 2 * channels] = dsec[:, half:]
@@ -332,15 +362,10 @@
         exchange(part_out, part_in, part_send, part_recv, step).start()
         return carry
 
-    lax.fori_loop(1, peers, scatter, 0)
+    loop(scatter)
     part_in[me] = part_out[me]
 
-    def take(step, carry):
-        _, got = arrival(part_in, part_send, part_recv, step)
-        got.wait()
-        return carry
-
-    lax.fori_loop(1, peers, take, 0)
+    drain(part_in, part_recv)
     total_out[...] = jnp.sum(part_in[...], axis=0)
 
     def spread(step):
@@ -348,8 +373,8 @@
         return pltpu.make_async_remote_copy(
             src_ref=total_out,
             dst_ref=total_in.at[me],
-            send_sem=total_send.at[peer],
-            recv_sem=total_recv.at[me],
+            send_sem=total_send,
+            recv_sem=total_recv,
             device_id={"slab": peer},
         )
 
@@ -357,19 +382,18 @@
         spread(step).start()
         return carry
 
-    lax.fori_loop(1, peers, give, 0)
+    loop(give)
     total_in[me] = total_out[...]
 
-    def collect(step, carry):
-        _, got = arrival(total_in, total_send, total_recv, step)
-        got.wait()
-        return carry
-
-    lax.fori_loop(1, peers, collect, 0)
+    drain(total_in, total_recv)
+    drain(want_in, want_send)
+    drain(reply_in, reply_send)
+    drain(part_in, part_send)
+    drain(total_in, total_send)
     for p in range(peers):
         flat_ref[p * share : (p + 1) * share] = total_in[p]
-    gsecond_ref[0:half] = flat_ref[0:channels].T
-    gsecond_ref[half:width] = flat_ref[channels : 2 * channels].T
+    gsecond_ref[:, 0:half] = flat_ref[0:channels]
+    gsecond_ref[:, half:width] = flat_ref[channels : 2 * channels]
     gfirst_ref[:, 0:half] = flat_ref[2 * channels : 2 * channels + 7]
     gfirst_ref[:, half:width] = flat_ref[2 * channels + 8 : 2 * channels + 15]
     glift_ref[...] = flat_ref[2 * channels + 16 : 2 * channels + 24, 0:channels]
@@ -399,13 +423,14 @@
     share = -(-(2 * channels + 24) // peers)
     span = GROUP * BLOCK_PTS
     vmem = pl.BlockSpec(memory_space=pltpu.VMEM)
-    sems = [pltpu.SemaphoreType.DMA((peers,))] * 8
-    return pl.pallas_call(
+    one = pltpu.SemaphoreType.DMA
+    sems = [one, pltpu.SemaphoreType.DMA((peers,))] + [one] * 6
+    latent, gfirst, gsecond, glift = pl.pallas_call(
         functools.partial(body, peers),
         out_shape=(
             jax.ShapeDtypeStruct((channels, cells), BF16),
             jax.ShapeDtypeStruct(w_first.shape, F32),
-            jax.ShapeDtypeStruct(w_second.shape, F32),
+            jax.ShapeDtypeStruct(w_second.shape[::-1], F32),
             jax.ShapeDtypeStruct(w_lift.shape, F32),
         ),
         in_specs=[vmem] * 4 + [pl.BlockSpec(memory_space=pltpu.SMEM)] + [vmem] * 5,
@@ -427,9 +452,11 @@
             pltpu.VMEM((width, span), F32),
             pltpu.VMEM((width, span), BF16),
             pltpu.VMEM((width, span), BF16),
+            pltpu.VMEM((32, span), BF16),
+            pltpu.VMEM((width, 32), BF16),
             pltpu.VMEM((channels, cells), F32),
             pltpu.VMEM((pairs, channels, BLOCK_PTS), F32),
-            pltpu.VMEM((channels, width), F32),
+            pltpu.VMEM((width, channels), F32),
             pltpu.VMEM((16, width), F32),
             pltpu.VMEM((peers * share, 128), F32),
             pltpu.VMEM((peers, share, 128), F32),
@@ -439,7 +466,7 @@
         ]
         + sems,
         compiler_params=pltpu.CompilerParams(
-            collective_id=0, has_side_effects=True, vmem_limit_bytes=40 * 1024 * 1024
+            collective_id=0, has_side_effects=True, vmem_limit_bytes=60 * 1024 * 1024
         ),
     )(
         point_pos,
@@ -449,10 +476,11 @@
         pair_cell,
         pair_mask,
         w_first,
-        w_second,
+        w_second.T,
         w_lift,
         cotangent,
     )
+    return latent, gfirst, gsecond.T, glift
 
 
 def solution(mesh):

time: 76.1 us -> 63.5 us (0.83)
  Pallas kernels: 67.8 us -> 58.6 us
  local copies, waits for them, and re-layouts: 7.3 us -> 4 us
    pallas_call x1, Pallas kernels: 67.8 us -> 58.6 us  [per_device(): pl.pallas_call(functools.partial(body, peers), out_shape=(jax.ShapeDtypeS...]
    unnamed x22 -> x8, local copies, waits for them, and re-layouts: 6.59 us -> 4 us
where the time goes in v2:
time: 63.5 us; the launch traced here: 63.3 us
  Pallas kernels  58.6 us (92%)
  local copies, waits for them, and re-layouts  4 us (6%)
  between operations  0.65 us (1%)
    pallas_call x1, Pallas kernels, per_device(): pl.pallas_call(functools.partial(body, peers), out_shape=(jax.ShapeDtypeS...  58.6 us
    unnamed x8, local copies, waits for them, and re-layouts  4 us

profile of v2, /device:TPU:0, one launch (start us, length us, event | category | flops | bytes accessed | tf_op | source)
XLA Modules:
  0.0 63.3 jit_solution(4145184493348342198)
XLA Ops:
  0.6 58.6 %shard_map.129 = (bf16[64,128]{1,0:T(8,128)(2,1)}, f32[7,256]{1,0:T(8,128)}, f32[64,256]{1,0:T(8,128)}, f32[8,64]{1,0:T(8,128)}) custom-call(f32[3,4096]{1,0:T(4,128)} %pos_ref.1, f32[8,4096]{1,0:T(8,128)} %input_ref.1, s32[1,512]{1,0:T(1,128)} %bitcast.6, s32[1,512]{1,0:T(1,128)} %bitcast.7, s32[4]{0:T(128)} %pair_ref.1, s32[4,64,128]{2,1,0:T(8,128)} %mask_ref.1, ...), custom_call_target="tpu_custom_call" | custom-call | tf_op jit(solution)/shard_map/pallas_call | solution.py:428
  59.3 0.0 copy-start
  59.3 1.3 %copy.18 = bf16[64,128]{1,0:T(8,128)(2,1)} copy(bf16[64,128]{1,0:T(8,128)(2,1)} %get-tuple-element.16) | data formatting | bytes 32768
  60.6 0.0 copy-done
  60.6 0.6 copy.19
  61.2 0.0 copy-start.1
  61.2 1.5 %copy.20 = f32[256,64]{0,1:T(8,128)} copy(f32[256,64]{0,1:T(8,128)} %bitcast.4) | data formatting | bytes 131072
  62.7 0.0 copy-done.1
  62.7 0.6 copy.21
Async XLA Ops:
  59.3 1.3 %copy-start = (f32[7,256]{1,0:T(8,128)S(1)}, f32[7,256]{1,0:T(8,128)}, u32[]{:S(2)}) copy-start(f32[7,256]{1,0:T(8,128)} %get-tuple-element.17) | copy-start | bytes 21508
  61.2 1.5 %copy-start.1 = (f32[8,64]{1,0:T(8,128)S(1)}, f32[8,64]{1,0:T(8,128)}, u32[]{:S(2)}) copy-start(f32[8,64]{1,0:T(8,128)} %get-tuple-element.19) | copy-start | bytes 6148

commit v3 on v2

--- a/solution.py
+++ b/solution.py
@@ -15,10 +15,9 @@
 GROUP = 8
 CHUNK = 64
 GELU_A = 0.7978845608028654
-GELU_B = 0.044715 * GELU_A
+GELU_B = 0.044715 / GELU_A**2
 
 ONE = np.array(1.0, ml_dtypes.bfloat16)
-A16 = np.array(GELU_A, ml_dtypes.bfloat16)
 B16 = np.array(GELU_B, ml_dtypes.bfloat16)
 C16 = np.array(3.0*GELU_B, ml_dtypes.bfloat16)
 PREC = lax.Precision.HIGHEST
@@ -73,10 +72,8 @@
     table_ref,
     reply_out,
     reply_in,
-    cellpart_ref,
     gcell_ref,
     cellrow_ref,
-    pointpart_ref,
     feat_ref,
     yrow_ref,
     dk_ref,
@@ -226,7 +223,6 @@
     row = (lax.div(index, GRID_ROW).astype(F32) + 0.5) * GRID_ROW / cells
     third = (me.astype(F32) + 0.5) / peers
     line = iota((16, cells), 0)
-    coords = jnp.where(line == 0, column, jnp.where(line == 1, row, third))
     shifted = jnp.where(
         line == 3,
         column,
@@ -235,17 +231,14 @@
         ),
     )
     first = first_ref[...]
-    cell_weights = jnp.concatenate([first[3:7], jnp.zeros((4, width), F32)], axis=0)
-    cell_values = jnp.where(line == 3, 1.0, jnp.where(line < 3, coords, 0.0))[0:8]
-    cellpart = tn_exact(cell_weights, cell_values)
     for k in range(blocks * groups):
         turn = (cells - k * GROUP) % cells
-        for value, into in ((cellpart, cellpart_ref), (gcells, gcell_ref), (shifted, cellrow_ref)):
+        for value, into in ((gcells, gcell_ref), (shifted, cellrow_ref)):
             into[k] = pltpu.roll(value, turn, 1) if turn else value
     half_turned = second_ref[...].astype(F32) * 0.5
     half_second = half_turned.T.astype(BF16)
     half_turned = half_turned.astype(BF16)
-    eight = jnp.concatenate([first, jnp.zeros((1, width), F32)], axis=0)
+    eight = jnp.concatenate([first, jnp.zeros((1, width), F32)], axis=0) * GELU_A
     coarse = eight.astype(BF16).astype(F32)
     wpre_ref[...] = jnp.concatenate(
         [
@@ -272,14 +265,11 @@
     gate = jax.nn.sigmoid(req_z)
     feats = req_z * gate
     slope = gate * (1.0 + req_z * (1.0 - gate))
-    point_weights = jnp.concatenate([first[0:3], jnp.zeros((5, width), F32)], axis=0)
-    pointpart = tn_exact(point_weights, points)
     upper = points.astype(BF16).astype(F32)
     both = jnp.concatenate([upper, points - upper], axis=0)
     for j in range(pairs):
         lanes = slice(j * BLOCK_PTS, (j + 1) * BLOCK_PTS)
         feat_ref[j] = feats[:, lanes]
-        pointpart_ref[j] = pointpart[:, lanes]
         yrow_ref[j] = both[:, lanes]
 
     def work(step, carry):
@@ -308,11 +298,11 @@
                 rows = slice(h, h + CHUNK)
                 x = pre[rows].astype(BF16)
                 square = x * x
-                t = jnp.tanh(x * (A16 + B16 * square))
+                t = jnp.tanh(x * (ONE + B16 * square))
                 u = ONE + t
                 hid = x * u
                 hid_ref[rows, both_lanes] = hid
-                bend = hid * (ONE - t) * (A16 + C16 * square)
+                bend = hid * (ONE - t) * (ONE + C16 * square)
                 dpre_ref[rows, both_lanes] = (u + bend) * dh_ref[rows, both_lanes].astype(BF16)
 
         def backward(s, lat, dfeat):
@@ -341,14 +331,14 @@
         dfir_ref[...] += nt(side_ref[0:16], dpre_ref[...])
         return carry
 
-    lax.fori_loop(0, pairs * groups, work, 0)
-
-    latent_ref[...] = (lat_ref[...] / divisor).astype(BF16)
-    dfeat = jnp.concatenate([dfeat_ref[j] for j in range(pairs)], axis=1)
+    lax.fori_loop(0, pairs * groups, work, 0, unroll=4)
+
+    latent_ref[...] = (lat_ref[...] / (divisor * GELU_A)).astype(BF16)
+    dfeat = jnp.concatenate([dfeat_ref[j] for j in range(pairs)], axis=1) * (1.0 / GELU_A)
     lift = nt(inputs, dfeat * slope, PREC)
     half = width // 2
     flat_ref[...] = jnp.zeros_like(flat_ref)
-    dsec = dsec_ref[...].T * 0.5
+    dsec = dsec_ref[...].T * (0.5 / GELU_A)
     dfir = dfir_ref[0:8] + dfir_ref[8:16]
     flat_ref[0:channels] = dsec[:, :half]
     flat_ref[channels : 2 * channels] = dsec[:, half:]
@@ -397,6 +387,11 @@
     gfirst_ref[:, 0:half] = flat_ref[2 * channels : 2 * channels + 7]
     gfirst_ref[:, half:width] = flat_ref[2 * channels + 8 : 2 * channels + 15]
     glift_ref[...] = flat_ref[2 * channels + 16 : 2 * channels + 24, 0:channels]
+
+
+def hand_out(*refs):
+    for source, target in zip(refs[:4], refs[4:]):
+        target[...] = source[...]
 
 
 def per_device(
@@ -442,10 +437,8 @@
             pltpu.VMEM((points // 128 * 16, 256), BF16),
             pltpu.VMEM((peers, rows, capacity), F32),
             pltpu.VMEM((peers, rows, capacity), F32),
-            pltpu.VMEM((kinds, width, cells), F32),
             pltpu.VMEM((kinds, channels, cells), F32),
             pltpu.VMEM((kinds, 16, cells), F32),
-            pltpu.VMEM((pairs, width, BLOCK_PTS), F32),
             pltpu.VMEM((pairs, channels, BLOCK_PTS), F32),
             pltpu.VMEM((pairs, 16, BLOCK_PTS), F32),
             pltpu.VMEM((channels, span), BF16),
@@ -480,6 +473,13 @@
         w_lift,
         cotangent,
     )
+    results = (latent, gfirst, gsecond, glift)
+    latent, gfirst, gsecond, glift = pl.pallas_call(
+        hand_out,
+        out_shape=tuple(jax.ShapeDtypeStruct(r.shape, r.dtype) for r in results),
+        in_specs=[vmem] * 4,
+        out_specs=[vmem] * 4,
+    )(*results)
     return latent, gfirst, gsecond.T, glift
 
 

time: 63.5 us -> 55.5 us (0.87)
  local copies, waits for them, and re-layouts: 4 us -> 0 us
  Pallas kernels: 58.6 us -> 54.7 us
    pallas_call x1, Pallas kernels: 58.6 us -> 53.2 us  [per_device(): pl.pallas_call(functools.partial(body, peers), out_shape=(jax.ShapeDtypeS...]
    unnamed x8 -> x0, local copies, waits for them, and re-layouts: 4 us -> none
    pallas_call x0 -> x1, Pallas kernels: none -> 1.52 us  [per_device(): pl.pallas_call(hand_out, out_shape=tuple((jax.ShapeDtypeStruct(r.shape, r...]
where the time goes in v3:
time: 55.5 us; the launch traced here: 55.3 us
  Pallas kernels  54.7 us (99%)
  between operations  0.64 us (1%)
    pallas_call x1, Pallas kernels, per_device(): pl.pallas_call(functools.partial(body, peers), out_shape=(jax.ShapeDtypeS...  53.2 us
    pallas_call x1, Pallas kernels, per_device(): pl.pallas_call(hand_out, out_shape=tuple((jax.ShapeDtypeStruct(r.shape, r...  1.52 us

profile of v3, /device:TPU:0, one launch (start us, length us, event | category | flops | bytes accessed | tf_op | source)
XLA Modules:
  0.0 55.3 jit_solution(12837652655198748800)
XLA Ops:
  0.6 53.2 %shard_map.129 = (bf16[64,128]{1,0:T(8,128)(2,1)}, f32[7,256]{1,0:T(8,128)}, f32[64,256]{1,0:T(8,128)}, f32[8,64]{1,0:T(8,128)}) custom-call(f32[3,4096]{1,0:T(4,128)} %pos_ref.1, f32[8,4096]{1,0:T(8,128)} %input_ref.1, s32[1,512]{1,0:T(1,128)} %bitcast.5, s32[1,512]{1,0:T(1,128)} %bitcast.6, s32[4]{0:T(128)} %pair_ref.1, s32[4,64,128]{2,1,0:T(8,128)} %mask_ref.1, ...), custom_call_target="tpu_custom_call" | custom-call | tf_op jit(solution)/shard_map/pallas_call | solution.py:423
  53.8 1.5 %shard_map.130 = (bf16[64,128]{1,0:T(8,128)(2,1)}, f32[7,256]{1,0:T(8,128)}, f32[64,256]{1,0:T(8,128)}, f32[8,64]{1,0:T(8,128)}) custom-call(bf16[64,128]{1,0:T(8,128)(2,1)} %get-tuple-element.12.refs_0_, f32[7,256]{1,0:T(8,128)} %get-tuple-element.13.refs_1_, f32[64,256]{1,0:T(8,128)} %get-tuple-element.14.refs_2_, f32[8,64]{1,0:T(8,128)} %get-tuple-element.15.refs_3_), custom_call_target="tpu_custom_call" | custom-call | tf_op jit(solution)/shard_map/pallas_call | solution.py:477
